TPU v7x, 256 devices: a whole 4x4x8 slice. The times are simulated.
256 devices in a mesh: layer: 16 (over z, x_hi), dp: 16 (over x_lo, y, core).
Axes of the slice: x: 4 (x_hi: 2, x_lo: 2; x = x_hi * 2 + x_lo), y: 4, z: 8, core: 2. Of those that a mesh axis runs over, the one named last changes fastest.
Arguments:
- query_grads: float32 [16, 1024, 4096], P('layer', 'dp'), may hold values from -6 to 6
- train_grads: float32 [16, 4096, 4096], P('layer', 'dp'), may hold values from -6 to 6
- eig_out: float32 [16, 64, 64], P('layer'), may hold values from -0.75 to 0.75
- eig_in: float32 [16, 64, 64], P('layer'), may hold values from -0.75 to 0.75
- eig_values: float32 [16, 4096], P('layer'), may hold values from 0.05 to 5
- train_ids: int32 [4096], P('dp'), may hold values from 0 to 9999999
Outputs:
- influence: float32 [1024, 4096], P('layer', 'dp')
All inputs are finite; a program needn't handle non-finite values.
Results may differ from a plain program's by a relative error of at most 0.0001.
Values sent between devices are 32-bit elements; how exact they have to be, the bound alone decides.
A program may use at most 192 MiB of HBM per device.

v0:
```python
import math

import jax
import jax.numpy as jnp
from jax import lax
from jax.sharding import PartitionSpec as P

CORPUS = 10000000


def rotate_all(grads, eig_out, eig_in):
    layers_here, count, flat = grads.shape
    rows_out = eig_out.shape[1]
    cols_in = eig_in.shape[1]
    shaped = grads.reshape(layers_here, count, rows_out, cols_in)
    turned = jnp.einsum("lnrc,lrs->lnsc", shaped, eig_out, precision=lax.Precision.HIGHEST)
    turned = jnp.einsum("lnsc,lct->lnst", turned, eig_in, precision=lax.Precision.HIGHEST)
    return turned.reshape(layers_here, count, flat)


def pair_scores(query_side, train_side):
    return jnp.einsum(
        "lnk,lmk->nm",
        query_side,
        train_side,
        precision=lax.Precision.HIGHEST,
        preferred_element_type=jnp.float32,
    )


def shards(query_grads, train_grads, eig_out, eig_in, eig_values, train_ids):
    layers_here = query_grads.shape[0]
    flat = query_grads.shape[2]
    damping = 0.1 * jnp.mean(eig_values, axis=1, keepdims=True)
    damped_inverse = 1.0 / (eig_values + damping)
    train_side = rotate_all(train_grads, eig_out, eig_in)
    scores = pair_scores(
        rotate_all(lax.all_gather(query_grads, "dp", axis=1, tiled=True), eig_out, eig_in)
        * damped_inverse[:, None, :],
        train_side,
    )
    summed = lax.psum_scatter(scores, "layer", scatter_dimension=0, tiled=True)
    position = train_ids.astype(jnp.float32) / float(CORPUS)
    rate = 0.1 + 0.45 * (1.0 + jnp.cos(jnp.pi * position))
    layer_count = layers_here * lax.axis_size("layer")
    return summed * rate[None, :] / math.sqrt(float(flat * layer_count))


def solution(mesh):
    placed = (
        P("layer", "dp", None),
        P("layer", "dp", None),
        P("layer", None, None),
        P("layer", None, None),
        P("layer", None),
        P("dp"),
    )
    return jax.shard_map(
        shards, mesh=mesh, in_specs=placed, out_specs=P("layer", "dp"), check_vma=False
    )
```

profile of v0, /device:TPU:34, one launch (start us, length us, event | category | flops | bytes accessed | tf_op | source)
XLA Modules:
  0.0 457.5 jit_solution(2790278200107904934)
XLA Ops:
  6.5 0.0 copy-start
  6.5 0.0 copy-start.3
  6.5 0.0 all-gather.2.cloned.1.call-start
  6.5 3.3 copy.16
  9.8 0.0 all-gather.2.cloned.1.call-update
  9.9 0.0 reduce-scatter.2.cloned.1.call-start
  9.9 5.6 %copy.22 = f32[1,256,4096]{1,2,0:T(8,128)} copy(f32[1,256,4096]{2,1,0:T(8,128)} %param.7) | data formatting | bytes 8388608 | tf_op args[1]
  15.5 1.4 reduce_sum.9
  17.5 0.8 divide_reduce_fusion
  18.3 0.1 mul.39
  18.4 0.0 copy-done
  18.4 8.4 %fusion.14 = f32[256,64,64]{0,1,2:T(8,128)S(1)} fusion(f32[256,64,64]{0,2,1:T(8,128)} %bitcast.34, f32[1,64,64]{2,1,0:T(8,128)S(1)} %copy-done), kind=kOutput, calls=%fused_computation.12 | convolution fusion | flops 805306368 | bytes 8404992 | tf_op jit(solution)/shard_map/lnrc,lrs->lnsc/dot_general | solution.py:16
  26.8 0.0 copy-done.3
  26.8 7.1 %fusion.10 = f32[256,64,64]{0,2,1:T(8,128)} fusion(f32[256,64,64]{0,1,2:T(8,128)S(1)} %fusion.14, f32[1,64,64]{2,1,0:T(8,128)S(1)} %copy-done.3), kind=kOutput, calls=%fused_computation.8 | convolution fusion | flops 805306368 | bytes 8404992 | tf_op jit(solution)/shard_map/lnsc,lct->lnst/dot_general | solution.py:17
  33.9 72.7 %all-gather.2.cloned.1.call-done = f32[1,1024,4096]{2,0,1:T(1,128)} async-done(((f32[1,64,4096]{2,0,1:T(1,128)}), f32[1,1024,4096]{2,0,1:T(1,128)}) %all-gather.2.cloned.1.call-update) | async-done | bytes 16777232 | tf_op jit(solution)/shard_map/all_gather | solution.py:38
  106.6 37.0 %copy.17 = f32[1,1024,4096]{1,2,0:T(8,128)} copy(f32[1,1024,4096]{2,0,1:T(1,128)} %all-gather.2.cloned.1.call-done) | data formatting | bytes 33554432 | tf_op jit(solution)/shard_map/all_gather | solution.py:38
  143.6 33.4 %fusion.6 = f32[1024,64,64]{0,1,2:T(8,128)} fusion(f32[1024,64,64]{0,2,1:T(8,128)} %bitcast.33, f32[1,64,64]{2,1,0:T(8,128)S(1)} %copy-done), kind=kOutput, calls=%fused_computation.6 | convolution fusion | flops 3221225472 | bytes 33570816 | tf_op jit(solution)/shard_map/lnrc,lrs->lnsc/dot_general | solution.py:16
  177.0 0.0 copy-start.2
  177.0 0.0 copy-start.1
  177.0 36.8 %fusion = f32[1024,64,64]{0,2,1:T(8,128)} fusion(f32[1024,64,64]{0,1,2:T(8,128)} %fusion.6, f32[1,64,64]{2,1,0:T(8,128)S(1)} %copy-done.3), kind=kOutput, calls=%fused_computation | convolution fusion | flops 3221225472 | bytes 33570816 | tf_op jit(solution)/shard_map/lnsc,lct->lnst/dot_general | solution.py:17
  213.8 0.0 copy-done.2
  213.8 0.0 copy-start.4
  213.8 32.9 %fusion.17 = f32[1024,256]{1,0:T(8,128)} fusion(f32[256,64,64]{0,2,1:T(8,128)S(1)} %copy-done.2, f32[1024,64,64]{0,2,1:T(8,128)} %fusion, f32[64,64]{1,0:T(8,128)S(1)} %mul.39), kind=kOutput, calls=%fused_computation.13 | convolution fusion | flops 12889096192 | bytes 22036480 | tf_op jit(solution)/shard_map/lnk,lmk->nm/dot_general | solution.py:22
  246.7 0.0 reduce-scatter.2.cloned.1.call-update
  246.7 0.0 copy-done.4
  246.8 202.2 %reduce-scatter.2.cloned.1.call-done = f32[64,256]{1,0:T(8,128)} async-done(((f32[1024,256]{1,0:T(8,128)}), f32[64,256]{1,0:T(8,128)}) %reduce-scatter.2.cloned.1.call-update) | async-done | bytes 65552 | tf_op jit(solution)/shard_map/reduce_scatter | solution.py:42
  449.0 1.5 multiply_multiply_fusion
  450.5 0.0 copy-done.1
  (1 shorter events, 0.0 us)
Async XLA Ops:
  6.5 11.8 %copy-start = (f32[1,64,64]{2,1,0:T(8,128)S(1)}, f32[1,64,64]{2,1,0:T(8,128)}, u32[]{:S(2)}) copy-start(f32[1,64,64]{2,1,0:T(8,128)} %param.8) | copy-start | bytes 49156
  6.5 20.3 %copy-start.3 = (f32[1,64,64]{2,1,0:T(8,128)S(1)}, f32[1,64,64]{2,1,0:T(8,128)}, u32[]{:S(2)}) copy-start(f32[1,64,64]{2,1,0:T(8,128)} %param.9) | copy-start | bytes 49156
  6.5 100.0 %all-gather.2.cloned.1.call-start = ((), (), s32[]{:S(2)}) async-start(), calls=%async_computation.1 | async-start | bytes 17825792 | tf_op jit(solution)/shard_map/all_gather | solution.py:38
  9.9 439.1 %reduce-scatter.2.cloned.1.call-start = ((), (), s32[]{:S(2)}) async-start(), calls=%async_computation.2 | async-start | bytes 1114112 | tf_op jit(solution)/shard_map/reduce_scatter | solution.py:42
  177.0 36.9 %copy-start.2 = (f32[256,64,64]{0,2,1:T(8,128)S(1)}, f32[256,64,64]{0,2,1:T(8,128)}, u32[]{:S(2)}) copy-start(f32[256,64,64]{0,2,1:T(8,128)} %fusion.10) | copy-start | bytes 12582916
  177.0 273.5 %copy-start.1 = (f32[1,64,64]{2,1,0:T(8,128)S(1)}, f32[1,64,64]{2,1,0:T(8,128)}, u32[]{:S(2)}) copy-start(f32[1,64,64]{2,1,0:T(8,128)} %param.8) | copy-start | bytes 49156
  213.8 32.9 %copy-start.4 = (s32[256]{0:T(256)S(1)}, s32[256]{0:T(256)}, u32[]{:S(2)}) copy-start(s32[256]{0:T(256)} %param.11) | copy-start | bytes 3076
Sparse Core Ops, SparseCore 0:
  10.0 96.5 all-gather.1
  246.8 202.1 reduce-scatter.1
where the time goes:
time: 467 us; the launch traced here: 458 us
  waiting for transfers between devices  275 us (59%)
  matrix products  119 us (25%)
  local copies, waits for them, and re-layouts  46 us (10%)
  between operations  14.3 us (3%)
    reduce_scatter x1, waiting for transfers between devices, shards(): summed = lax.psum_scatter(scores, 'layer', scatter_dimension=0, tiled=True)  202 us
    all_gather x1, waiting for transfers between devices, shards(): lax.all_gather(query_grads, 'dp', axis=1, tiled=True)  72.7 us
    dot_general x2, matrix products, rotate_all(): jnp.einsum('lnsc,lct->lnst', turned, eig_in, precision=lax.Precision.HIGH...  43.9 us
    dot_general x2, matrix products, rotate_all(): jnp.einsum('lnrc,lrs->lnsc', shaped, eig_out, precision=lax.Precision.HIG...  41.8 us
    all_gather x1, local copies, waits for them, and re-layouts, shards(): lax.all_gather(query_grads, 'dp', axis=1, tiled=True)  37 us
    dot_general x1, matrix products, pair_scores(): jnp.einsum('lnk,lmk->nm', query_side, train_side, precision=lax.Precision...  32.9 us
  transfers between devices with their start and end apart: 2, of which 2 were waited for; matrix products, arithmetic and copies ran while one was open for 5% of the time, Pallas kernels for 0%

commit v1 on v0

v1 whole, which is shorter than its diff:
```python
import functools
import math

import jax
import jax.numpy as jnp
from jax import lax
from jax.experimental import pallas as pl
from jax.experimental.pallas import tpu as pltpu
from jax.sharding import PartitionSpec as P

CORPUS = 10000000
MESH = pl.DeviceIdType.MESH
PIECES = 4

STEPS = ((0, 0), (0, 1), (0, -1), (1, 0), (0, 2), (1, 1), (1, -1), (1, 2))


def split(value):
    high = value.astype(jnp.bfloat16)
    low = (value - high.astype(jnp.float32)).astype(jnp.bfloat16)
    return high, low


def kernel(q_ref, t_ref, o_ref, held, t_land, t_hi, t_lo, q_hi, q_lo, scores, landed,
           load_sem, t_sem, send_sem, half_sem, recv_sem, out_sem, in_sem):
    layer = lax.axis_index("layer")
    dp = lax.axis_index("dp")
    core, y, x = dp % 2, (dp // 2) % 4, dp // 8
    count = q_ref.shape[0]
    rows = count // PIECES
    half = rows // 2
    layers = landed.shape[0]

    def place(dx, dy, dc):
        return (((x + dx) % 2) * 4 + (y + dy + 4) % 4) * 2 + (core + dc) % 2

    x_flip, y_up, y_down, twin = place(1, 0, 0), place(0, 1, 0), place(0, -1, 0), place(0, 0, 1)

    barrier = pltpu.get_barrier_semaphore()
    for other in (x_flip, y_up, y_down, twin):
        pl.semaphore_signal(barrier, inc=1, device_id={"dp": other}, device_id_type=MESH)

    @pl.loop(1, layers)
    def _(step):
        pl.semaphore_signal(barrier, inc=1, device_id={"layer": (layer + step) % layers}, device_id_type=MESH)

    own = pltpu.make_async_copy(q_ref, held.at[0], load_sem)
    own.start()
    t_load = pltpu.make_async_copy(t_ref, t_land, t_sem)
    t_load.start()
    own.wait()
    pl.semaphore_wait(barrier, 4 + layers - 1)

    def send(slot, piece, target, to_slot, kind, first=0, size=None, from_sem=None, arrival=None):
        size = rows if size is None else size
        window = pl.ds(pl.multiple_of(piece * rows + first, 8), size)
        pltpu.make_async_remote_copy(
            src_ref=held.at[slot, window, :],
            dst_ref=held.at[to_slot, window, :],
            send_sem=send_sem.at[kind] if from_sem is None else from_sem,
            recv_sem=recv_sem.at[to_slot if arrival is None else arrival, piece],
            device_id={"dp": target},
            device_id_type=MESH,
        ).start()

    def arrive(slot, piece, first=0, size=None, arrival=None):
        size = rows if size is None else size
        window = pl.ds(pl.multiple_of(piece * rows + first, 8), size)
        block = held.at[slot, window, :]
        pltpu.make_async_copy(block, block, recv_sem.at[slot if arrival is None else arrival, piece]).wait()

    @pl.loop(0, PIECES)
    def _(piece):
        send(0, piece, y_up, 1, 0)
        send(0, piece, y_down, 2, 1)
        send(0, piece, x_flip, 3, 2)
        send(0, piece, twin, 8, 8)

    t_load.wait()
    tiles = 16
    t_rows = t_ref.shape[0] // tiles

    @pl.loop(0, tiles)
    def _(tile):
        window = pl.ds(pl.multiple_of(tile * t_rows, 16), t_rows)
        t_hi[window, :], t_lo[window, :] = split(t_land[window, :])

    def relay_near(piece):
        arrive(1, piece)
        send(1, piece, y_up, 4, None, 0, half, half_sem.at[0])
        send(1, piece, twin, 9, 9)
        arrive(2, piece)
        send(2, piece, y_down, 4, None, half, half, half_sem.at[1], 16)
        send(2, piece, twin, 10, 10)
        arrive(3, piece)
        send(3, piece, y_up, 5, 3)
        send(3, piece, y_down, 6, 4)
        send(3, piece, twin, 11, 11)

    def relay_far(piece):
        arrive(4, piece, 0, half)
        arrive(4, piece, half, half, 16)
        send(4, piece, x_flip, 7, 5)
        send(4, piece, twin, 12, 12)
        arrive(5, piece)
        send(5, piece, twin, 13, 13)
        arrive(6, piece)
        send(6, piece, twin, 14, 14)

    def finish(piece):
        arrive(7, piece)
        send(7, piece, twin, 15, 15)
        window = pl.ds(pl.multiple_of(piece * rows, 8), rows)

        for slot in range(16):
            if slot >= 8:
                arrive(slot, piece)
            to = pl.ds(slot * rows, rows)
            q_hi[to, :], q_lo[to, :] = split(held[slot, window, :])
        dims = (((1,), (1,)), ((), ()))
        product = functools.partial(lax.dot_general, dimension_numbers=dims, preferred_element_type=jnp.float32)
        scores[piece] = (
            product(q_hi[...], t_lo[...]) + product(q_lo[...], t_hi[...]) + product(q_hi[...], t_hi[...])
        )
        for slot in range(16):
            dx, dy = STEPS[slot % 8]
            owner = place(dx, -dy, slot // 8)
            block = scores.at[piece, pl.ds(slot * rows, rows), :]
            to = landed.at[layer, window, :]

            @pl.when(owner != layer)
            def _():
                pltpu.make_async_remote_copy(
                    src_ref=block, dst_ref=to, send_sem=out_sem.at[slot], recv_sem=in_sem.at[layer],
                    device_id={"layer": owner}, device_id_type=MESH,
                ).start()

            @pl.when(owner == layer)
            def _():
                landed[layer, window, :] = scores[piece, pl.ds(slot * rows, rows), :]

    @pl.loop(0, PIECES + 2)
    def _(step):
        @pl.when(step < PIECES)
        def _():
            relay_near(step)

        @pl.when((step >= 1) & (step < PIECES + 1))
        def _():
            relay_far(step - 1)

        @pl.when(step >= 2)
        def _():
            finish(step - 2)

    o_ref[...] = landed[layer]

    @pl.loop(1, layers)
    def _(step):
        peer = (layer + step) % layers
        block = landed.at[peer]
        pltpu.make_async_copy(block, block, in_sem.at[peer]).wait()
        o_ref[...] += landed[peer]

    for kind in range(16):
        if kind not in (6, 7):
            pltpu.make_async_copy(held.at[0], held.at[0], send_sem.at[kind]).wait()
    for kind in range(2):
        block = held.at[0, pl.ds(0, count // 2), :]
        pltpu.make_async_copy(block, block, half_sem.at[kind]).wait()
    for slot in range(16):
        dx, dy = STEPS[slot % 8]
        owner = place(dx, -dy, slot // 8)

        @pl.when(owner != layer)
        def _():
            pltpu.make_async_copy(landed.at[0], landed.at[0], out_sem.at[slot]).wait()


def transform(grads, eig_out, eig_in, damped_inverse):
    count, flat = grads.shape
    side_out, side_in = eig_out.shape[0], eig_in.shape[0]
    turn = functools.partial(jnp.einsum, precision=lax.Precision.HIGHEST)
    turned = turn("nrc,rs->nsc", grads.reshape(count, side_out, side_in), eig_out)
    turned = turn("nsc,ct->nst", turned, eig_in)
    turned = turned * damped_inverse.reshape(side_out, side_in)[None]
    turned = turn("nst,ct->nsc", turned, eig_in)
    turned = turn("nsc,rs->nrc", turned, eig_out)
    return turned.reshape(count, flat)


def shards(query_grads, train_grads, eig_out, eig_in, eig_values, train_ids):
    query, train = query_grads[0], train_grads[0]
    count, flat = query.shape
    t_count = train.shape[0]
    layers = lax.axis_size("layer")
    everyone = lax.axis_size("dp") * count
    damping = 0.1 * jnp.mean(eig_values[0])
    back = transform(query, eig_out[0], eig_in[0], 1.0 / (eig_values[0] + damping))
    rows = count // PIECES
    total = pl.pallas_call(
        kernel,
        out_shape=jax.ShapeDtypeStruct((count, t_count), jnp.float32),
        in_specs=[pl.BlockSpec(memory_space=pl.ANY)] * 2,
        out_specs=pl.BlockSpec(memory_space=pltpu.VMEM),
        scratch_shapes=[
            pltpu.VMEM((16, count, flat), jnp.float32),
            pltpu.VMEM((t_count, flat), jnp.float32),
            pltpu.VMEM((t_count, flat), jnp.bfloat16),
            pltpu.VMEM((t_count, flat), jnp.bfloat16),
            pltpu.VMEM((16 * rows, flat), jnp.bfloat16),
            pltpu.VMEM((16 * rows, flat), jnp.bfloat16),
            pltpu.VMEM((PIECES, 16 * rows, t_count), jnp.float32),
            pltpu.VMEM((layers, count, t_count), jnp.float32),
            pltpu.SemaphoreType.DMA,
            pltpu.SemaphoreType.DMA,
            pltpu.SemaphoreType.DMA((16,)),
            pltpu.SemaphoreType.DMA((2,)),
            pltpu.SemaphoreType.DMA((17, PIECES)),
            pltpu.SemaphoreType.DMA((16,)),
            pltpu.SemaphoreType.DMA((layers,)),
        ],
        compiler_params=pltpu.CompilerParams(
            collective_id=0, has_side_effects=True, vmem_limit_bytes=56 * 1024 * 1024
        ),
        cost_estimate=pl.CostEstimate(
            flops=6 * everyone * t_count * flat, bytes_accessed=4 * flat * (count + t_count), transcendentals=0
        ),
    )(back, train)
    position = train_ids.astype(jnp.float32) / float(CORPUS)
    rate = 0.1 + 0.45 * (1.0 + jnp.cos(jnp.pi * position))
    return total * rate[None, :] / math.sqrt(float(flat * layers))


def solution(mesh):
    placed = (
        P("layer", "dp", None),
        P("layer", "dp", None),
        P("layer", None, None),
        P("layer", None, None),
        P("layer", None),
        P("dp"),
    )
    return jax.shard_map(
        shards, mesh=mesh, in_specs=placed, out_specs=P("layer", "dp"), check_vma=False
    )
```

time: 467 us -> 111 us (0.24)
  the two profiles are of different devices: /device:TPU:34 before, /device:TPU:6 now
where the time goes in v1:
time: 111 us
  Pallas kernels  89.9 us (81%)
  matrix products  11.5 us (10%)
  local copies, waits for them, and re-layouts  6.88 us (6%)
  other arithmetic  2.21 us (2%)
    pallas_call x1, Pallas kernels, shards(): pl.pallas_call(kernel, out_shape=jax.ShapeDtypeStruct((count, t_count), j...  89.9 us
    dot_general x1, matrix products, transform(): turned = turn('nst,ct->nsc', turned, eig_in)  6.08 us
    reshape x1, local copies, waits for them, and re-layouts, transform(): return turned.reshape(count, flat)  2.9 us

profile of v1, /device:TPU:6, one launch (start us, length us, event | category | flops | bytes accessed | tf_op | source)
XLA Modules:
  0.0 111.3 jit_solution(9441640225821435050)
XLA Ops:
  0.0 0.0 copy-start
  0.0 0.0 copy-start.1
  0.0 2.0 %reshape_squeeze.3 = f32[64,64,64]{2,1,0:T(8,128)S(1)} reshape(f32[1,64,4096]{2,1,0:T(8,128)} %param.6) | data formatting | bytes 2097152 | tf_op jit(solution)/shard_map/reshape;squeeze | solution.py:184
  2.0 0.0 copy-done.1
  2.0 1.9 %fusion.8 = f32[64,64,64]{2,0,1:T(8,128)S(1)} fusion(f32[64,64,64]{2,1,0:T(8,128)S(1)} %reshape_squeeze.3, f32[1,64,64]{2,1,0:T(8,128)S(1)} %copy-done.1), kind=kOutput, calls=%fused_computation.10 | convolution fusion | flops 201326592 | bytes 2113536 | tf_op jit(solution)/shard_map/nrc,rs->nsc/dot_general | solution.py:184
  4.0 0.0 copy-done
  4.0 0.0 copy-start.2
  4.0 1.8 %fusion = f32[64,64,64]{2,1,0:T(8,128)S(1)} fusion(f32[64,64,64]{2,0,1:T(8,128)S(1)} %fusion.8, f32[1,64,64]{2,1,0:T(8,128)S(1)} %copy-done), kind=kOutput, calls=%fused_computation | convolution fusion | flops 201326592 | bytes 2113536 | tf_op jit(solution)/shard_map/nsc,ct->nst/dot_general | solution.py:185
  5.8 0.0 copy-done.2
  5.8 0.6 reduce_sum.9
  7.1 0.1 div.24
  7.2 6.1 %fusion.2 = f32[64,64,64]{1,2,0:T(8,128)S(1)} fusion(f32[64,64,64]{2,1,0:T(8,128)S(1)} %fusion, f32[64,64]{1,0:T(8,128)S(1)} %div.24, f32[1,64,64]{2,1,0:T(8,128)S(1)} %copy-done), kind=kOutput, calls=%fused_computation.2 | convolution fusion | flops 201588736 | bytes 2129920 | tf_op jit(solution)/shard_map/nst,ct->nsc/dot_general | solution.py:187
  13.3 1.8 %convolution_bitcast_fusion = f32[64,64,64]{1,2,0:T(8,128)S(1)} fusion(f32[64,64,64]{1,2,0:T(8,128)S(1)} %fusion.2, f32[1,64,64]{2,1,0:T(8,128)S(1)} %copy-done.1), kind=kOutput, calls=%fused_computation.4 | convolution fusion | flops 201326592 | bytes 2113536 | tf_op jit(solution)/shard_map/nsc,rs->nrc/dot_general | solution.py:188
  15.1 1.9 %copy.7 = f32[64,64,64]{2,1,0:T(8,128)} copy(f32[64,64,64]{1,2,0:T(8,128)S(1)} %convolution_bitcast_fusion) | data formatting | bytes 2097152 | tf_op jit(solution)/shard_map/nsc,rs->nrc/transpose | solution.py:188
  16.9 2.9 %reshape.14.q_ref = f32[64,4096]{1,0:T(8,128)} reshape(f32[64,64,64]{2,1,0:T(8,128)} %copy.7) | data formatting | bytes 2097152 | tf_op jit(solution)/shard_map/reshape | solution.py:189
  19.8 0.0 copy-start.3
  19.8 89.9 %shard_map.64 = f32[64,256]{1,0:T(8,128)} custom-call(f32[64,4096]{1,0:T(8,128)} %reshape.14.q_ref, f32[256,4096]{1,0:T(8,128)} %bitcast.21), custom_call_target="tpu_custom_call" | custom-call | flops 6442450944 | bytes 5242880 | tf_op jit(solution)/shard_map/pallas_call | solution.py:201
  109.8 0.0 copy-done.3
  109.8 1.5 %multiply_multiply_fusion = f32[64,256]{1,0:T(8,128)} fusion(f32[64,256]{1,0:T(8,128)} %shard_map.64, f32[256]{0:T(256)S(1)} %multiply_add_fusion), kind=kLoop, calls=%fused_computation.6 | loop fusion | flops 32768 | bytes 132096 | tf_op jit(solution)/shard_map/div | solution.py:232
  (2 shorter events, 0.1 us)
Async XLA Ops:
  0.0 4.0 %copy-start = (f32[1,64,64]{2,1,0:T(8,128)S(1)}, f32[1,64,64]{2,1,0:T(8,128)}, u32[]{:S(2)}) copy-start(f32[1,64,64]{2,1,0:T(8,128)} %param.9) | copy-start | bytes 49156
  0.0 2.0 %copy-start.1 = (f32[1,64,64]{2,1,0:T(8,128)S(1)}, f32[1,64,64]{2,1,0:T(8,128)}, u32[]{:S(2)}) copy-start(f32[1,64,64]{2,1,0:T(8,128)} %param.8) | copy-start | bytes 49156
  4.0 1.8 %copy-start.2 = (f32[1,4096]{1,0:T(1,128)S(1)}, f32[1,4096]{1,0:T(1,128)}, u32[]{:S(2)}) copy-start(f32[1,4096]{1,0:T(1,128)} %param.10) | copy-start | bytes 49156
  19.8 89.9 %copy-start.3 = (s32[256]{0:T(256)S(1)}, s32[256]{0:T(256)}, u32[]{:S(2)}) copy-start(s32[256]{0:T(256)} %param.11) | copy-start | bytes 3076

commit v2 on v0

v2 whole, which is shorter than its diff:
```python
import functools
import math

import jax
import jax.numpy as jnp
from jax import lax
from jax.experimental import pallas as pl
from jax.experimental.pallas import tpu as pltpu
from jax.sharding import PartitionSpec as P

CORPUS = 10000000
MESH = pl.DeviceIdType.MESH
ROWS = 8
GROUP = 16
PACK = 4

STEPS = ((0, 0), (0, 1), (0, -1), (1, 0), (0, 2), (1, 1), (1, -1), (1, 2))


def split(value):
    high = value.astype(jnp.bfloat16)
    low = (value - high.astype(jnp.float32)).astype(jnp.bfloat16)
    return high, low


def product(left, right, flipped=False):
    dims = (((1,), (1 if flipped else 0,)), ((), ()))
    dot = functools.partial(lax.dot_general, dimension_numbers=dims, preferred_element_type=jnp.float32)
    return dot(left[0], right[1]) + dot(left[1], right[0]) + dot(left[0], right[0])


def stack(flat):
    wide = PACK * 64
    return jnp.concatenate([flat[:, wide * i:wide * (i + 1)] for i in range(flat.shape[1] // wide)], axis=0)


def unstack(stacked):
    return jnp.concatenate([stacked[ROWS * i:ROWS * (i + 1), :] for i in range(stacked.shape[0] // ROWS)], axis=1)


def to_columns(stacked):
    turned = stacked.T
    side = turned.shape[0] // PACK
    return jnp.concatenate([turned[side * j:side * (j + 1), :] for j in range(PACK)], axis=1)


def from_columns(columns):
    wide = columns.shape[1] // PACK
    return jnp.concatenate([columns[:, wide * j:wide * (j + 1)] for j in range(PACK)], axis=0).T


def spread(basis, size, index, lane):
    side = basis.shape[0]
    iota = functools.partial(lax.broadcasted_iota, jnp.int32)
    tall = (index(iota((size, side), 0)) == iota((size, side), 1)).astype(jnp.bfloat16)
    wide = (iota((side, size), 0) == index(iota((side, size), 1))).astype(jnp.bfloat16)
    same = lane(iota((size, size), 0)) == lane(iota((size, size), 1))
    dot = functools.partial(jnp.dot, preferred_element_type=jnp.float32)
    return [
        jnp.where(same, dot(dot(tall, part).astype(jnp.bfloat16), wide), 0.0).astype(jnp.bfloat16)
        for part in split(basis)
    ]


def rotate(grads, out_op, in_op, inverse):
    parts = grads.shape[0] // ROWS
    tall = stack(grads[:ROWS]).shape[0]

    def each(turn, value, size):
        return jnp.concatenate([turn(value[size * k:size * (k + 1)]) for k in range(parts)], axis=0)

    value = each(stack, grads, ROWS)
    value = product(split(value), in_op)
    value = each(to_columns, value, tall)
    value = product(split(value), out_op)
    value = value * jnp.concatenate([inverse] * parts, axis=0)
    value = product(split(value), out_op, True)
    value = each(from_columns, value, 64)
    value = product(split(value), in_op, True)
    return each(unstack, value, tall)


def kernel(q_ref, t_ref, eig_out_ref, eig_in_ref, values_ref, o_ref,
           held, q_land, t_land, t_hi, t_lo, q_hi, q_lo, out_hi, out_lo, in_hi, in_lo, inverse,
           scores, landed, sums, crossed, load_sem, t_sem, send_sem, recv_sem, out_sem, in_sem, cross_sem):
    layer = lax.axis_index("layer")
    dp = lax.axis_index("dp")
    core, y, x = dp % 2, (dp // 2) % 4, dp // 8
    z, side = layer // 2, layer % 2
    count = q_ref.shape[0]
    pieces = count // ROWS
    depth = landed.shape[1]

    def place(dx, dy, dc):
        return (((x + dx) % 2) * 4 + (y + dy + 4) % 4) * 2 + (core + dc) % 2

    x_flip, y_up, y_down, twin = place(1, 0, 0), place(0, 1, 0), place(0, -1, 0), place(0, 0, 1)
    across = z * 2 + 1 - side

    load = pltpu.make_async_copy(q_ref, q_land, load_sem)
    load.start()
    t_load = pltpu.make_async_copy(t_ref, t_land, t_sem)
    t_load.start()

    barrier = pltpu.get_barrier_semaphore()
    for other in (x_flip, y_up, y_down, twin):
        pl.semaphore_signal(barrier, inc=1, device_id={"dp": other}, device_id_type=MESH)
    pl.semaphore_signal(barrier, inc=1, device_id={"layer": across}, device_id_type=MESH)

    @pl.loop(1, depth)
    def _(step):
        other = ((z + step) % depth) * 2 + side
        pl.semaphore_signal(barrier, inc=1, device_id={"layer": other}, device_id_type=MESH)

    def send(slot, piece, target, to_slot, kind):
        window = pl.ds(pl.multiple_of(piece * ROWS, ROWS), ROWS)
        pltpu.make_async_remote_copy(
            src_ref=held.at[slot, window, :],
            dst_ref=held.at[to_slot, window, :],
            send_sem=send_sem.at[kind],
            recv_sem=recv_sem.at[to_slot, piece],
            device_id={"dp": target},
            device_id_type=MESH,
        ).start()

    def to_twin(slot, piece):
        send(slot, piece, twin, 8 + slot, 9 + slot)

    def arrive(slot, piece):
        block = held.at[slot, pl.ds(pl.multiple_of(piece * ROWS, ROWS), ROWS), :]
        pltpu.make_async_copy(block, block, recv_sem.at[slot, piece]).wait()

    out_hi[...], out_lo[...] = spread(
        eig_out_ref[...], out_hi.shape[0], lambda a: (a % 128) // ROWS * PACK + a // 128, lambda a: a % ROWS
    )
    in_hi[...], in_lo[...] = spread(eig_in_ref[...], in_hi.shape[0], lambda a: a % 64, lambda a: a // 64)
    values = values_ref[...]
    damped = 1.0 / (values + 0.1 * jnp.mean(values))
    inverse[...] = to_columns(stack(jnp.broadcast_to(damped, (ROWS, damped.shape[1]))))

    load.wait()

    @pl.loop(0, count // GROUP)
    def _(group):
        window = pl.ds(pl.multiple_of(group * GROUP, GROUP), GROUP)
        held[0, window, :] = rotate(
            q_land[window, :], (out_hi[...], out_lo[...]), (in_hi[...], in_lo[...]), inverse[...]
        )

        @pl.when(group == 0)
        def _():
            pl.semaphore_wait(barrier, 5 + depth - 1)

        for k in range(GROUP // ROWS):
            piece = group * (GROUP // ROWS) + k
            send(0, piece, y_up, 1, 0)
            send(0, piece, y_down, 2, 1)
            send(0, piece, x_flip, 3, 2)
            to_twin(0, piece)

    t_load.wait()
    t_count = t_ref.shape[0]

    @pl.loop(0, t_ref.shape[1] // t_count)
    def _(tile):
        window = pl.ds(pl.multiple_of(tile * t_count, t_count), t_count)
        t_hi[window, :], t_lo[window, :] = split(t_land[:, window].T)

    def relay_near(piece):
        way = piece % 3
        arrive(1, piece)

        @pl.when(way != 1)
        def _():
            send(1, piece, y_up, 4, 3)

        @pl.when(way == 2)
        def _():
            send(1, piece, x_flip, 5, 5)

        to_twin(1, piece)
        arrive(2, piece)

        @pl.when(way == 1)
        def _():
            send(2, piece, y_down, 4, 4)

        to_twin(2, piece)
        arrive(3, piece)

        @pl.when(way != 2)
        def _():
            send(3, piece, y_up, 5, 6)

        send(3, piece, y_down, 6, 7)
        to_twin(3, piece)

    def relay_far(piece):
        arrive(4, piece)
        send(4, piece, x_flip, 7, 8)
        to_twin(4, piece)
        arrive(5, piece)
        to_twin(5, piece)
        arrive(6, piece)
        to_twin(6, piece)

    def score(piece):
        arrive(7, piece)
        to_twin(7, piece)
        window = pl.ds(pl.multiple_of(piece * ROWS, ROWS), ROWS)
        for slot in range(8, 16):
            arrive(slot, piece)
        for slot in range(8):
            to = pl.ds(slot * 2 * ROWS, 2 * ROWS)
            both = jnp.concatenate([held[slot, window, :], held[8 + slot, window, :]], axis=0)
            q_hi[to, :], q_lo[to, :] = split(both)
        scores[piece] = product((q_hi[...], q_lo[...]), (t_hi[...], t_lo[...]))
        for slot in range(8):
            dx, dy = STEPS[slot]
            owner = place(dx, -dy, 0) // 2
            block = scores.at[piece, pl.ds(slot * 2 * ROWS, 2 * ROWS), :]

            @pl.when(owner != z)
            def _():
                pltpu.make_async_remote_copy(
                    src_ref=block, dst_ref=landed.at[piece, z], send_sem=out_sem.at[slot], recv_sem=in_sem.at[piece],
                    device_id={"layer": owner * 2 + side}, device_id_type=MESH,
                ).start()

            @pl.when(owner == z)
            def _():
                landed[piece, z] = scores[piece, pl.ds(slot * 2 * ROWS, 2 * ROWS), :]

    kept = (core + side) % 2

    def gather_depth(piece):
        block = landed.at[piece, pl.ds(0, depth - 1)]
        pltpu.make_async_copy(block, block, in_sem.at[piece]).wait()
        sums[piece] = jnp.sum(landed[piece], axis=0)
        pltpu.make_async_remote_copy(
            src_ref=sums.at[piece, pl.ds(pl.multiple_of((1 - kept) * ROWS, ROWS), ROWS), :],
            dst_ref=crossed.at[piece],
            send_sem=cross_sem.at[0], recv_sem=cross_sem.at[1],
            device_id={"layer": across}, device_id_type=MESH,
        ).start()

    @pl.loop(0, pieces + 4)
    def _(step):
        @pl.when(step < pieces)
        def _():
            relay_near(step)

        @pl.when((step >= 2) & (step < pieces + 2))
        def _():
            relay_far(step - 2)

        @pl.when((step >= 3) & (step < pieces + 3))
        def _():
            score(step - 3)

        @pl.when(step >= 4)
        def _():
            gather_depth(step - 4)

    pltpu.make_async_copy(crossed, crossed, cross_sem.at[1]).wait()

    @pl.loop(0, pieces)
    def _(piece):
        window = pl.ds(pl.multiple_of(piece * ROWS, ROWS), ROWS)
        mine = pl.ds(pl.multiple_of(kept * ROWS, ROWS), ROWS)
        o_ref[window, :] = sums[piece, mine, :] + crossed[piece]

    pltpu.make_async_copy(crossed, crossed, cross_sem.at[0]).wait()
    by_way = [len([piece for piece in range(pieces) if piece % 3 == way]) for way in range(3)]
    sent = {3: by_way[0] + by_way[2], 4: by_way[1], 5: by_way[2], 6: by_way[0] + by_way[1]}
    for kind in range(17):
        block = held.at[0, pl.ds(0, sent.get(kind, pieces) * ROWS), :]
        pltpu.make_async_copy(block, block, send_sem.at[kind]).wait()
    for slot in range(8):
        dx, dy = STEPS[slot]
        owner = place(dx, -dy, 0) // 2

        @pl.when(owner != z)
        def _():
            block = landed.at[:, 0]
            pltpu.make_async_copy(block, block, out_sem.at[slot]).wait()


def shards(query_grads, train_grads, eig_out, eig_in, eig_values, train_ids):
    query, train = query_grads[0], train_grads[0]
    count, flat = query.shape
    t_count = train.shape[0]
    layers = lax.axis_size("layer")
    everyone = lax.axis_size("dp") * count
    pieces = count // ROWS
    side = eig_out.shape[1]
    f32, bf16 = jnp.float32, jnp.bfloat16
    vmem = pl.BlockSpec(memory_space=pltpu.VMEM)
    total = pl.pallas_call(
        kernel,
        out_shape=jax.ShapeDtypeStruct((count, t_count), f32),
        in_specs=[pl.BlockSpec(memory_space=pl.ANY)] * 2 + [vmem] * 3,
        out_specs=vmem,
        scratch_shapes=[
            pltpu.VMEM((16, count, flat), f32),
            pltpu.VMEM((count, flat), f32),
            pltpu.VMEM((t_count, flat), f32),
            pltpu.VMEM((flat, t_count), bf16),
            pltpu.VMEM((flat, t_count), bf16),
            pltpu.VMEM((16 * ROWS, flat), bf16),
            pltpu.VMEM((16 * ROWS, flat), bf16),
            pltpu.VMEM((side * ROWS, side * ROWS), bf16),
            pltpu.VMEM((side * ROWS, side * ROWS), bf16),
            pltpu.VMEM((side * PACK, side * PACK), bf16),
            pltpu.VMEM((side * PACK, side * PACK), bf16),
            pltpu.VMEM((side, side * ROWS), f32),
            pltpu.VMEM((pieces, 16 * ROWS, t_count), f32),
            pltpu.VMEM((pieces, layers // 2, 2 * ROWS, t_count), f32),
            pltpu.VMEM((pieces, 2 * ROWS, t_count), f32),
            pltpu.VMEM((pieces, ROWS, t_count), f32),
            pltpu.SemaphoreType.DMA,
            pltpu.SemaphoreType.DMA,
            pltpu.SemaphoreType.DMA((17,)),
            pltpu.SemaphoreType.DMA((16, pieces)),
            pltpu.SemaphoreType.DMA((8,)),
            pltpu.SemaphoreType.DMA((pieces,)),
            pltpu.SemaphoreType.DMA((2,)),
        ],
        compiler_params=pltpu.CompilerParams(
            collective_id=0, has_side_effects=True, vmem_limit_bytes=56 * 1024 * 1024
        ),
        cost_estimate=pl.CostEstimate(
            flops=6 * everyone * t_count * flat, bytes_accessed=4 * flat * (count + t_count), transcendentals=0
        ),
    )(query, train, eig_out[0], eig_in[0], eig_values)
    position = train_ids.astype(f32) / float(CORPUS)
    rate = 0.1 + 0.45 * (1.0 + jnp.cos(jnp.pi * position))
    return total * rate[None, :] / math.sqrt(float(flat * layers))


def solution(mesh):
    placed = (
        P("layer", "dp", None),
        P("layer", "dp", None),
        P("layer", None, None),
        P("layer", None, None),
        P("layer", None),
        P("dp"),
    )
    return jax.shard_map(
        shards, mesh=mesh, in_specs=placed, out_specs=P("layer", "dp"), check_vma=False
    )
```

time: 467 us -> 91.7 us (0.20); the launches traced: 458 us -> 90.1 us
  waiting for transfers between devices: 275 us -> 0 us
  matrix products: 119 us -> 0 us
  Pallas kernels: 0 us -> 87.9 us
  local copies, waits for them, and re-layouts: 46 us -> 0 us
  between operations: 14.3 us -> 0.01 us
    reduce_scatter x1 -> x0, waiting for transfers between devices: 202 us -> none  [shards(): summed = lax.psum_scatter(scores, 'layer', scatter_dimension=0, tiled=True)]
    dot_general x5 -> x0, matrix products: 119 us -> none  [the longest x2 43.9 us: rotate_all(): jnp.einsum('lnsc,lct->lnst', turned, eig_in, precision=lax.Precision.HIGH...]
    pallas_call x0 -> x1, Pallas kernels: none -> 87.9 us  [shards(): pl.pallas_call(kernel, out_shape=jax.ShapeDtypeStruct((count, t_count), f...]
    all_gather x1 -> x0, waiting for transfers between devices: 72.7 us -> none  [shards(): lax.all_gather(query_grads, 'dp', axis=1, tiled=True)]
    all_gather x1 -> x0, local copies, waits for them, and re-layouts: 37 us -> none  [shards(): lax.all_gather(query_grads, 'dp', axis=1, tiled=True)]
    unnamed x12 -> x0, local copies, waits for them, and re-layouts: 8.93 us -> none
  transfers between devices with their start and end apart: 2 -> 0, of which waited for: 2 -> 0; matrix products, arithmetic and copies ran while one was open for 5% -> 0% of each run, Pallas kernels for 0% -> 0%
where the time goes in v2:
time: 91.7 us; the launch traced here: 90.1 us
  Pallas kernels  87.9 us (96%)
  other arithmetic  2.2 us (2%)
    pallas_call x1, Pallas kernels, shards(): pl.pallas_call(kernel, out_shape=jax.ShapeDtypeStruct((count, t_count), f...  87.9 us

profile of v2, /device:TPU:34, one launch (start us, length us, event | category | flops | bytes accessed | tf_op | source)
XLA Modules:
  0.0 90.1 jit_solution(3867001910214257435)
XLA Ops:
  0.0 0.7 multiply_add_fusion
  0.7 87.9 %shard_map.64 = f32[64,256]{1,0:T(8,128)} custom-call(f32[64,4096]{1,0:T(8,128)} %bitcast.5, f32[256,4096]{1,0:T(8,128)} %bitcast.4, f32[64,64]{1,0:T(8,128)} %bitcast.6, f32[64,64]{1,0:T(8,128)} %bitcast.7, f32[1,4096]{1,0:T(1,128)} %values_ref.1), custom_call_target="tpu_custom_call" | custom-call | flops 6442450944 | bytes 5242880 | tf_op jit(solution)/shard_map/pallas_call | solution.py:299
  88.7 1.5 %multiply_multiply_fusion = f32[64,256]{1,0:T(8,128)} fusion(f32[64,256]{1,0:T(8,128)} %shard_map.64, f32[256]{0:T(256)S(1)} %multiply_add_fusion), kind=kLoop, calls=%fused_computation | loop fusion | flops 32768 | bytes 132096 | tf_op jit(solution)/shard_map/div | solution.py:338

commit v3 on v2

--- a/solution.py
+++ b/solution.py
@@ -80,9 +80,9 @@
     return each(unstack, value, tall)
 
 
-def kernel(q_ref, t_ref, eig_out_ref, eig_in_ref, values_ref, o_ref,
-           held, q_land, t_land, t_hi, t_lo, q_hi, q_lo, out_hi, out_lo, in_hi, in_lo, inverse,
-           scores, landed, sums, crossed, load_sem, t_sem, send_sem, recv_sem, out_sem, in_sem, cross_sem):
+def kernel(q_ref, t_ref, eig_out_ref, eig_in_ref, values_ref, ids_ref, o_ref,
+           held, q_land, weight, t_land, t_hi, t_lo, q_hi, q_lo, out_hi, out_lo, in_hi, in_lo, inverse,
+           scores, landed, direct, sums, crossed, load_sem, t_sem, send_sem, recv_sem, out_sem, in_sem, cross_sem):
     layer = lax.axis_index("layer")
     dp = lax.axis_index("dp")
     core, y, x = dp % 2, (dp // 2) % 4, dp // 8
@@ -90,6 +90,8 @@
     count = q_ref.shape[0]
     pieces = count // ROWS
     depth = landed.shape[1]
+    last = pieces - 1
+    layers = direct.shape[0]
 
     def place(dx, dy, dc):
         return (((x + dx) % 2) * 4 + (y + dy + 4) % 4) * 2 + (core + dc) % 2
@@ -100,17 +102,14 @@
     load = pltpu.make_async_copy(q_ref, q_land, load_sem)
     load.start()
     t_load = pltpu.make_async_copy(t_ref, t_land, t_sem)
-    t_load.start()
 
     barrier = pltpu.get_barrier_semaphore()
     for other in (x_flip, y_up, y_down, twin):
         pl.semaphore_signal(barrier, inc=1, device_id={"dp": other}, device_id_type=MESH)
-    pl.semaphore_signal(barrier, inc=1, device_id={"layer": across}, device_id_type=MESH)
-
-    @pl.loop(1, depth)
+
+    @pl.loop(1, layers)
     def _(step):
-        other = ((z + step) % depth) * 2 + side
-        pl.semaphore_signal(barrier, inc=1, device_id={"layer": other}, device_id_type=MESH)
+        pl.semaphore_signal(barrier, inc=1, device_id={"layer": (layer + step) % layers}, device_id_type=MESH)
 
     def send(slot, piece, target, to_slot, kind):
         window = pl.ds(pl.multiple_of(piece * ROWS, ROWS), ROWS)
@@ -139,6 +138,7 @@
     inverse[...] = to_columns(stack(jnp.broadcast_to(damped, (ROWS, damped.shape[1]))))
 
     load.wait()
+    t_load.start()
 
     @pl.loop(0, count // GROUP)
     def _(group):
@@ -149,7 +149,7 @@
 
         @pl.when(group == 0)
         def _():
-            pl.semaphore_wait(barrier, 5 + depth - 1)
+            pl.semaphore_wait(barrier, 4 + layers - 1)
 
         for k in range(GROUP // ROWS):
             piece = group * (GROUP // ROWS) + k
@@ -158,6 +158,10 @@
             send(0, piece, x_flip, 3, 2)
             to_twin(0, piece)
 
+    position = ids_ref[...].astype(jnp.float32) / float(CORPUS)
+    rate = 0.1 + 0.45 * (1.0 + jnp.cos(jnp.pi * position))
+    weight[...] = rate / math.sqrt(float(q_ref.shape[1] * landed.shape[1] * 2))
+
     t_load.wait()
     t_count = t_ref.shape[0]
 
@@ -166,7 +170,7 @@
         window = pl.ds(pl.multiple_of(tile * t_count, t_count), t_count)
         t_hi[window, :], t_lo[window, :] = split(t_land[:, window].T)
 
-    def relay_near(piece):
+    def relay_rows(piece):
         way = piece % 3
         arrive(1, piece)
 
@@ -186,9 +190,11 @@
             send(2, piece, y_down, 4, 4)
 
         to_twin(2, piece)
+
+    def relay_flip(piece):
         arrive(3, piece)
 
-        @pl.when(way != 2)
+        @pl.when(piece % 3 != 2)
         def _():
             send(3, piece, y_up, 5, 6)
 
@@ -199,37 +205,53 @@
         arrive(4, piece)
         send(4, piece, x_flip, 7, 8)
         to_twin(4, piece)
-        arrive(5, piece)
-        to_twin(5, piece)
-        arrive(6, piece)
-        to_twin(6, piece)
-
-    def score(piece):
-        arrive(7, piece)
-        to_twin(7, piece)
+
+    def share_last(piece):
+        for slot in (7, 5, 6):
+            arrive(slot, piece)
+            to_twin(slot, piece)
+
+    def score(piece, part):
         window = pl.ds(pl.multiple_of(piece * ROWS, ROWS), ROWS)
-        for slot in range(8, 16):
-            arrive(slot, piece)
-        for slot in range(8):
-            to = pl.ds(slot * 2 * ROWS, 2 * ROWS)
+        slots = range(4 * part, 4 * part + 4)
+        for slot in slots:
+            arrive(8 + slot, piece)
+        for at, slot in enumerate(slots):
+            to = pl.ds(at * 2 * ROWS, 2 * ROWS)
             both = jnp.concatenate([held[slot, window, :], held[8 + slot, window, :]], axis=0)
             q_hi[to, :], q_lo[to, :] = split(both)
-        scores[piece] = product((q_hi[...], q_lo[...]), (t_hi[...], t_lo[...]))
-        for slot in range(8):
+        scores[piece, part] = product((q_hi[...], q_lo[...]), (t_hi[...], t_lo[...]))
+        for at, slot in enumerate(slots):
             dx, dy = STEPS[slot]
             owner = place(dx, -dy, 0) // 2
-            block = scores.at[piece, pl.ds(slot * 2 * ROWS, 2 * ROWS), :]
-
-            @pl.when(owner != z)
+
+            @pl.when((piece < last) & (owner != z))
             def _():
                 pltpu.make_async_remote_copy(
-                    src_ref=block, dst_ref=landed.at[piece, z], send_sem=out_sem.at[slot], recv_sem=in_sem.at[piece],
+                    src_ref=scores.at[piece, part, pl.ds(at * 2 * ROWS, 2 * ROWS), :], dst_ref=landed.at[piece, z],
+                    send_sem=out_sem.at[0], recv_sem=in_sem.at[piece],
                     device_id={"layer": owner * 2 + side}, device_id_type=MESH,
                 ).start()
 
-            @pl.when(owner == z)
+            @pl.when((piece < last) & (owner == z))
             def _():
-                landed[piece, z] = scores[piece, pl.ds(slot * 2 * ROWS, 2 * ROWS), :]
+                landed[piece, z] = scores[piece, part, pl.ds(at * 2 * ROWS, 2 * ROWS), :]
+
+            for other in range(2):
+                target = owner * 2 + (core + other) % 2
+                block = pl.ds((at * 2 + other) * ROWS, ROWS)
+
+                @pl.when((piece == last) & (target != layer))
+                def _():
+                    pltpu.make_async_remote_copy(
+                        src_ref=scores.at[last, part, block, :], dst_ref=direct.at[layer],
+                        send_sem=out_sem.at[1], recv_sem=in_sem.at[last],
+                        device_id={"layer": target}, device_id_type=MESH,
+                    ).start()
+
+                @pl.when((piece == last) & (target == layer))
+                def _():
+                    direct[layer] = scores[last, part, block, :]
 
     kept = (core + side) % 2
 
@@ -244,46 +266,42 @@
             device_id={"layer": across}, device_id_type=MESH,
         ).start()
 
-    @pl.loop(0, pieces + 4)
+    stages = (
+        (0, relay_rows),
+        (2, relay_flip),
+        (3, lambda piece: score(piece, 0)),
+        (5, relay_far),
+        (8, share_last),
+        (9, lambda piece: score(piece, 1)),
+    )
+
+    @pl.loop(0, pieces + stages[-1][0])
     def _(step):
-        @pl.when(step < pieces)
-        def _():
-            relay_near(step)
-
-        @pl.when((step >= 2) & (step < pieces + 2))
-        def _():
-            relay_far(step - 2)
-
-        @pl.when((step >= 3) & (step < pieces + 3))
-        def _():
-            score(step - 3)
-
-        @pl.when(step >= 4)
-        def _():
-            gather_depth(step - 4)
-
-    pltpu.make_async_copy(crossed, crossed, cross_sem.at[1]).wait()
-
-    @pl.loop(0, pieces)
-    def _(piece):
-        window = pl.ds(pl.multiple_of(piece * ROWS, ROWS), ROWS)
-        mine = pl.ds(pl.multiple_of(kept * ROWS, ROWS), ROWS)
-        o_ref[window, :] = sums[piece, mine, :] + crossed[piece]
-
-    pltpu.make_async_copy(crossed, crossed, cross_sem.at[0]).wait()
+        for behind, stage in stages:
+            pl.when((step >= behind) & (step < pieces + behind))(functools.partial(stage, step - behind))
+
     by_way = [len([piece for piece in range(pieces) if piece % 3 == way]) for way in range(3)]
     sent = {3: by_way[0] + by_way[2], 4: by_way[1], 5: by_way[2], 6: by_way[0] + by_way[1]}
     for kind in range(17):
         block = held.at[0, pl.ds(0, sent.get(kind, pieces) * ROWS), :]
         pltpu.make_async_copy(block, block, send_sem.at[kind]).wait()
-    for slot in range(8):
-        dx, dy = STEPS[slot]
-        owner = place(dx, -dy, 0) // 2
-
-        @pl.when(owner != z)
-        def _():
-            block = landed.at[:, 0]
-            pltpu.make_async_copy(block, block, out_sem.at[slot]).wait()
+
+    pl.loop(0, last)(gather_depth)
+    pltpu.make_async_copy(crossed, crossed, cross_sem.at[1]).wait()
+
+    @pl.loop(0, last)
+    def _(piece):
+        window = pl.ds(pl.multiple_of(piece * ROWS, ROWS), ROWS)
+        mine = pl.ds(pl.multiple_of(kept * ROWS, ROWS), ROWS)
+        o_ref[window, :] = (sums[piece, mine, :] + crossed[piece]) * weight[...]
+
+    pltpu.make_async_copy(crossed, crossed, cross_sem.at[0]).wait()
+    block = landed.at[:, pl.ds(0, depth - 1)]
+    pltpu.make_async_copy(block, block, out_sem.at[0]).wait()
+    block = direct.at[pl.ds(0, direct.shape[0] - 1)]
+    pltpu.make_async_copy(block, block, out_sem.at[1]).wait()
+    pltpu.make_async_copy(block, block, in_sem.at[last]).wait()
+    o_ref[pl.ds(last * ROWS, ROWS), :] = jnp.sum(direct[...], axis=0) * weight[...]
 
 
 def shards(query_grads, train_grads, eig_out, eig_in, eig_values, train_ids):
@@ -296,33 +314,35 @@
     side = eig_out.shape[1]
     f32, bf16 = jnp.float32, jnp.bfloat16
     vmem = pl.BlockSpec(memory_space=pltpu.VMEM)
-    total = pl.pallas_call(
+    return pl.pallas_call(
         kernel,
         out_shape=jax.ShapeDtypeStruct((count, t_count), f32),
-        in_specs=[pl.BlockSpec(memory_space=pl.ANY)] * 2 + [vmem] * 3,
+        in_specs=[pl.BlockSpec(memory_space=pl.ANY)] * 2 + [vmem] * 4,
         out_specs=vmem,
         scratch_shapes=[
             pltpu.VMEM((16, count, flat), f32),
             pltpu.VMEM((count, flat), f32),
+            pltpu.VMEM((1, t_count), f32),
             pltpu.VMEM((t_count, flat), f32),
             pltpu.VMEM((flat, t_count), bf16),
             pltpu.VMEM((flat, t_count), bf16),
-            pltpu.VMEM((16 * ROWS, flat), bf16),
-            pltpu.VMEM((16 * ROWS, flat), bf16),
+            pltpu.VMEM((8 * ROWS, flat), bf16),
+            pltpu.VMEM((8 * ROWS, flat), bf16),
             pltpu.VMEM((side * ROWS, side * ROWS), bf16),
             pltpu.VMEM((side * ROWS, side * ROWS), bf16),
             pltpu.VMEM((side * PACK, side * PACK), bf16),
             pltpu.VMEM((side * PACK, side * PACK), bf16),
             pltpu.VMEM((side, side * ROWS), f32),
-            pltpu.VMEM((pieces, 16 * ROWS, t_count), f32),
-            pltpu.VMEM((pieces, layers // 2, 2 * ROWS, t_count), f32),
-            pltpu.VMEM((pieces, 2 * ROWS, t_count), f32),
-            pltpu.VMEM((pieces, ROWS, t_count), f32),
+            pltpu.VMEM((pieces, 2, 8 * ROWS, t_count), f32),
+            pltpu.VMEM((pieces - 1, layers // 2, 2 * ROWS, t_count), f32),
+            pltpu.VMEM((layers, ROWS, t_count), f32),
+            pltpu.VMEM((pieces - 1, 2 * ROWS, t_count), f32),
+            pltpu.VMEM((pieces - 1, ROWS, t_count), f32),
             pltpu.SemaphoreType.DMA,
             pltpu.SemaphoreType.DMA,
             pltpu.SemaphoreType.DMA((17,)),
             pltpu.SemaphoreType.DMA((16, pieces)),
-            pltpu.SemaphoreType.DMA((8,)),
+            pltpu.SemaphoreType.DMA((2,)),
             pltpu.SemaphoreType.DMA((pieces,)),
             pltpu.SemaphoreType.DMA((2,)),
         ],
@@ -332,10 +352,7 @@
         cost_estimate=pl.CostEstimate(
             flops=6 * everyone * t_count * flat, bytes_accessed=4 * flat * (count + t_count), transcendentals=0
         ),
-    )(query, train, eig_out[0], eig_in[0], eig_values)
-    position = train_ids.astype(f32) / float(CORPUS)
-    rate = 0.1 + 0.45 * (1.0 + jnp.cos(jnp.pi * position))
-    return total * rate[None, :] / math.sqrt(float(flat * layers))
+    )(query, train, eig_out[0], eig_in[0], eig_values, train_ids[None])
 
 
 def solution(mesh):

time: 91.7 us -> 84 us (0.916); the launches traced: 90.1 us -> 83.8 us
  Pallas kernels: 87.9 us -> 82.3 us
  other arithmetic: 2.2 us -> 0 us
  local copies, waits for them, and re-layouts: 0 us -> 1.47 us
    pallas_call x1, Pallas kernels: 87.9 us -> 82.3 us  [shards(): pl.pallas_call(kernel, out_shape=jax.ShapeDtypeStruct((count, t_count), f...]
    div x1 -> x0, other arithmetic: 1.48 us -> none  [shards(): return total * rate[None, :] / math.sqrt(float(flat * layers))]
    unnamed x0 -> x1, local copies, waits for them, and re-layouts: none -> 1.47 us
where the time goes in v3:
time: 84 us; the launch traced here: 83.8 us
  Pallas kernels  82.3 us (98%)
  local copies, waits for them, and re-layouts  1.47 us (2%)
    pallas_call x1, Pallas kernels, shards(): pl.pallas_call(kernel, out_shape=jax.ShapeDtypeStruct((count, t_count), f...  82.3 us

profile of v3, /device:TPU:34, one launch (start us, length us, event | category | flops | bytes accessed | tf_op | source)
XLA Modules:
  0.0 83.8 jit_solution(11325336133018867291)
XLA Ops:
  0.0 82.3 %shard_map.64 = f32[64,256]{1,0:T(8,128)} custom-call(f32[64,4096]{1,0:T(8,128)} %bitcast.6, f32[256,4096]{1,0:T(8,128)} %bitcast.5, f32[64,64]{1,0:T(8,128)} %bitcast.7, f32[64,64]{1,0:T(8,128)} %bitcast.8, f32[1,4096]{1,0:T(1,128)} %values_ref.1, s32[1,256]{1,0:T(1,128)} %bitcast.9), custom_call_target="tpu_custom_call" | custom-call | flops 6442450944 | bytes 5242880 | tf_op jit(solution)/shard_map/pallas_call | solution.py:317
  82.3 1.5 %copy.8 = f32[64,256]{1,0:T(8,128)} copy(f32[64,256]{1,0:T(8,128)} %shard_map.64) | data formatting | bytes 131072

commit v4 on v3

--- a/solution.py
+++ b/solution.py
@@ -1,5 +1,6 @@
 import functools
 import math
+import operator
 
 import jax
 import jax.numpy as jnp
@@ -12,6 +13,7 @@
 MESH = pl.DeviceIdType.MESH
 ROWS = 8
 GROUP = 16
+WAYS = (0, 1, 2, 1, 0, 2, 1, 0)
 PACK = 4
 
 STEPS = ((0, 0), (0, 1), (0, -1), (1, 0), (0, 2), (1, 1), (1, -1), (1, 2))
@@ -122,11 +124,19 @@
             device_id_type=MESH,
         ).start()
 
-    def to_twin(slot, piece):
-        send(slot, piece, twin, 8 + slot, 9 + slot)
-
-    def arrive(slot, piece):
-        block = held.at[slot, pl.ds(pl.multiple_of(piece * ROWS, ROWS), ROWS), :]
+    def to_twin(slot, piece, slots=1):
+        window = pl.ds(pl.multiple_of(piece * ROWS, ROWS), ROWS)
+        pltpu.make_async_remote_copy(
+            src_ref=held.at[pl.ds(slot, slots), window, :],
+            dst_ref=held.at[pl.ds(8 + slot, slots), window, :],
+            send_sem=send_sem.at[9 + slot],
+            recv_sem=recv_sem.at[8 + slot, piece],
+            device_id={"dp": twin},
+            device_id_type=MESH,
+        ).start()
+
+    def arrive(slot, piece, slots=1):
+        block = held.at[pl.ds(slot, slots), pl.ds(pl.multiple_of(piece * ROWS, ROWS), ROWS), :]
         pltpu.make_async_copy(block, block, recv_sem.at[slot, piece]).wait()
 
     out_hi[...], out_lo[...] = spread(
@@ -170,31 +180,32 @@
         window = pl.ds(pl.multiple_of(tile * t_count, t_count), t_count)
         t_hi[window, :], t_lo[window, :] = split(t_land[:, window].T)
 
+    def goes(piece, way):
+        return functools.reduce(operator.or_, [piece == at for at in range(pieces) if WAYS[at] == way])
+
     def relay_rows(piece):
-        way = piece % 3
         arrive(1, piece)
 
-        @pl.when(way != 1)
+        @pl.when(jnp.logical_not(goes(piece, 1)))
         def _():
             send(1, piece, y_up, 4, 3)
 
-        @pl.when(way == 2)
+        @pl.when(goes(piece, 2))
         def _():
             send(1, piece, x_flip, 5, 5)
 
-        to_twin(1, piece)
         arrive(2, piece)
 
-        @pl.when(way == 1)
+        @pl.when(goes(piece, 1))
         def _():
             send(2, piece, y_down, 4, 4)
 
-        to_twin(2, piece)
+        to_twin(1, piece, 2)
 
     def relay_flip(piece):
         arrive(3, piece)
 
-        @pl.when(piece % 3 != 2)
+        @pl.when(jnp.logical_not(goes(piece, 2)))
         def _():
             send(3, piece, y_up, 5, 6)
 
@@ -207,20 +218,25 @@
         to_twin(4, piece)
 
     def share_last(piece):
-        for slot in (7, 5, 6):
-            arrive(slot, piece)
-            to_twin(slot, piece)
-
-    def score(piece, part):
+        arrive(7, piece)
+        to_twin(7, piece)
+        arrive(5, piece)
+        arrive(6, piece)
+        to_twin(5, piece, 2)
+
+    def take(piece, part):
         window = pl.ds(pl.multiple_of(piece * ROWS, ROWS), ROWS)
-        slots = range(4 * part, 4 * part + 4)
-        for slot in slots:
-            arrive(8 + slot, piece)
-        for at, slot in enumerate(slots):
-            to = pl.ds(at * 2 * ROWS, 2 * ROWS)
+        for slot, slots in ((8 + 4 * part, 1), (9 + 4 * part, 2), (11 + 4 * part, 1)):
+            arrive(slot, piece, slots)
+        for at in range(4):
+            slot = 4 * part + at
+            to = pl.ds(slot * 2 * ROWS, 2 * ROWS)
             both = jnp.concatenate([held[slot, window, :], held[8 + slot, window, :]], axis=0)
             q_hi[to, :], q_lo[to, :] = split(both)
-        scores[piece, part] = product((q_hi[...], q_lo[...]), (t_hi[...], t_lo[...]))
+
+    def give(piece, part, both):
+        scores[piece, part] = both[part * 8 * ROWS:(part + 1) * 8 * ROWS]
+        slots = range(4 * part, 4 * part + 4)
         for at, slot in enumerate(slots):
             dx, dy = STEPS[slot]
             owner = place(dx, -dy, 0) // 2
@@ -266,24 +282,27 @@
             device_id={"layer": across}, device_id_type=MESH,
         ).start()
 
-    stages = (
-        (0, relay_rows),
-        (2, relay_flip),
-        (3, lambda piece: score(piece, 0)),
-        (5, relay_far),
-        (8, share_last),
-        (9, lambda piece: score(piece, 1)),
-    )
-
-    @pl.loop(0, pieces + stages[-1][0])
+    stages = ((0, relay_rows), (1, relay_flip), (5, relay_far), (6, share_last))
+    score_behind = (6, 7)
+
+    @pl.loop(0, pieces + score_behind[1])
     def _(step):
         for behind, stage in stages:
             pl.when((step >= behind) & (step < pieces + behind))(functools.partial(stage, step - behind))
 
-    by_way = [len([piece for piece in range(pieces) if piece % 3 == way]) for way in range(3)]
+        @pl.when(step >= score_behind[0])
+        def _():
+            valid = [(step >= behind) & (step < pieces + behind) for behind in score_behind]
+            for part in range(2):
+                pl.when(valid[part])(functools.partial(take, step - score_behind[part], part))
+            both = product((q_hi[...], q_lo[...]), (t_hi[...], t_lo[...]))
+            for part in (1, 0):
+                pl.when(valid[part])(functools.partial(give, step - score_behind[part], part, both))
+
+    by_way = [WAYS.count(way) for way in range(3)]
     sent = {3: by_way[0] + by_way[2], 4: by_way[1], 5: by_way[2], 6: by_way[0] + by_way[1]}
-    for kind in range(17):
-        block = held.at[0, pl.ds(0, sent.get(kind, pieces) * ROWS), :]
+    for kind in [kind for kind in range(17) if kind not in (11, 15)]:
+        block = held.at[pl.ds(0, 2 if kind in (10, 14) else 1), pl.ds(0, sent.get(kind, pieces) * ROWS), :]
         pltpu.make_async_copy(block, block, send_sem.at[kind]).wait()
 
     pl.loop(0, last)(gather_depth)
@@ -326,8 +345,8 @@
             pltpu.VMEM((t_count, flat), f32),
             pltpu.VMEM((flat, t_count), bf16),
             pltpu.VMEM((flat, t_count), bf16),
-            pltpu.VMEM((8 * ROWS, flat), bf16),
-            pltpu.VMEM((8 * ROWS, flat), bf16),
+            pltpu.VMEM((16 * ROWS, flat), bf16),
+            pltpu.VMEM((16 * ROWS, flat), bf16),
             pltpu.VMEM((side * ROWS, side * ROWS), bf16),
             pltpu.VMEM((side * ROWS, side * ROWS), bf16),
             pltpu.VMEM((side * PACK, side * PACK), bf16),

time: 84 us -> 81.5 us (0.970); the launches traced: 83.8 us -> 80.4 us
  Pallas kernels: 82.3 us -> 78.9 us
    pallas_call x1, Pallas kernels: 82.3 us -> 78.9 us  [shards(): pl.pallas_call(kernel, out_shape=jax.ShapeDtypeStruct((count, t_count), f...]
where the time goes in v4:
time: 81.5 us; the launch traced here: 80.4 us
  Pallas kernels  78.9 us (97%)
  local copies, waits for them, and re-layouts  1.47 us (2%)
    pallas_call x1, Pallas kernels, shards(): pl.pallas_call(kernel, out_shape=jax.ShapeDtypeStruct((count, t_count), f...  78.9 us

profile of v4, /device:TPU:34, one launch (start us, length us, event | category | flops | bytes accessed | tf_op | source)
XLA Modules:
  0.0 80.4 jit_solution(3254676667796896366)
XLA Ops:
  0.0 78.9 %shard_map.64 = f32[64,256]{1,0:T(8,128)} custom-call(f32[64,4096]{1,0:T(8,128)} %bitcast.6, f32[256,4096]{1,0:T(8,128)} %bitcast.5, f32[64,64]{1,0:T(8,128)} %bitcast.7, f32[64,64]{1,0:T(8,128)} %bitcast.8, f32[1,4096]{1,0:T(1,128)} %values_ref.1, s32[1,256]{1,0:T(1,128)} %bitcast.9), custom_call_target="tpu_custom_call" | custom-call | flops 6442450944 | bytes 5242880 | tf_op jit(solution)/shard_map/pallas_call | solution.py:336
  78.9 1.5 %copy.8 = f32[64,256]{1,0:T(8,128)} copy(f32[64,256]{1,0:T(8,128)} %shard_map.64) | data formatting | bytes 131072

commit v5 on v4

--- a/solution.py
+++ b/solution.py
@@ -82,7 +82,8 @@
     return each(unstack, value, tall)
 
 
-def kernel(q_ref, t_ref, eig_out_ref, eig_in_ref, values_ref, ids_ref, o_ref,
+def kernel(q_ref, t_ref, eig_out_hbm, eig_in_hbm, values_hbm, ids_hbm, o_ref,
+           eig_out_ref, eig_in_ref, values_ref, ids_ref, small_sem,
            held, q_land, weight, t_land, t_hi, t_lo, q_hi, q_lo, out_hi, out_lo, in_hi, in_lo, inverse,
            scores, landed, direct, sums, crossed, load_sem, t_sem, send_sem, recv_sem, out_sem, in_sem, cross_sem):
     layer = lax.axis_index("layer")
@@ -101,17 +102,25 @@
     x_flip, y_up, y_down, twin = place(1, 0, 0), place(0, 1, 0), place(0, -1, 0), place(0, 0, 1)
     across = z * 2 + 1 - side
 
+    barrier = pltpu.get_barrier_semaphore()
+    for other in (x_flip, y_up, y_down, twin):
+        pl.semaphore_signal(barrier, inc=1, device_id={"dp": other}, device_id_type=MESH)
+
+    @pl.loop(1, layers)
+    def _(step):
+        pl.semaphore_signal(barrier, inc=1, device_id={"layer": (layer + step) % layers}, device_id_type=MESH)
+
+    small = [
+        pltpu.make_async_copy(source, target, small_sem.at[at])
+        for at, (source, target) in enumerate((
+            (eig_out_hbm, eig_out_ref), (eig_in_hbm, eig_in_ref), (values_hbm, values_ref), (ids_hbm, ids_ref)
+        ))
+    ]
+    for copy in small:
+        copy.start()
     load = pltpu.make_async_copy(q_ref, q_land, load_sem)
     load.start()
     t_load = pltpu.make_async_copy(t_ref, t_land, t_sem)
-
-    barrier = pltpu.get_barrier_semaphore()
-    for other in (x_flip, y_up, y_down, twin):
-        pl.semaphore_signal(barrier, inc=1, device_id={"dp": other}, device_id_type=MESH)
-
-    @pl.loop(1, layers)
-    def _(step):
-        pl.semaphore_signal(barrier, inc=1, device_id={"layer": (layer + step) % layers}, device_id_type=MESH)
 
     def send(slot, piece, target, to_slot, kind):
         window = pl.ds(pl.multiple_of(piece * ROWS, ROWS), ROWS)
@@ -124,8 +133,8 @@
             device_id_type=MESH,
         ).start()
 
-    def to_twin(slot, piece, slots=1):
-        window = pl.ds(pl.multiple_of(piece * ROWS, ROWS), ROWS)
+    def to_twin(slot, piece, slots=1, span=1):
+        window = pl.ds(pl.multiple_of(piece * ROWS, ROWS), span * ROWS)
         pltpu.make_async_remote_copy(
             src_ref=held.at[pl.ds(slot, slots), window, :],
             dst_ref=held.at[pl.ds(8 + slot, slots), window, :],
@@ -135,10 +144,12 @@
             device_id_type=MESH,
         ).start()
 
-    def arrive(slot, piece, slots=1):
-        block = held.at[pl.ds(slot, slots), pl.ds(pl.multiple_of(piece * ROWS, ROWS), ROWS), :]
+    def arrive(slot, piece, slots=1, span=1):
+        block = held.at[pl.ds(slot, slots), pl.ds(pl.multiple_of(piece * ROWS, ROWS), span * ROWS), :]
         pltpu.make_async_copy(block, block, recv_sem.at[slot, piece]).wait()
 
+    for copy in small:
+        copy.wait()
     out_hi[...], out_lo[...] = spread(
         eig_out_ref[...], out_hi.shape[0], lambda a: (a % 128) // ROWS * PACK + a // 128, lambda a: a % ROWS
     )
@@ -150,8 +161,7 @@
     load.wait()
     t_load.start()
 
-    @pl.loop(0, count // GROUP)
-    def _(group):
+    def own(group):
         window = pl.ds(pl.multiple_of(group * GROUP, GROUP), GROUP)
         held[0, window, :] = rotate(
             q_land[window, :], (out_hi[...], out_lo[...]), (in_hi[...], in_lo[...]), inverse[...]
@@ -166,7 +176,10 @@
             send(0, piece, y_up, 1, 0)
             send(0, piece, y_down, 2, 1)
             send(0, piece, x_flip, 3, 2)
-            to_twin(0, piece)
+
+        to_twin(0, group * (GROUP // ROWS), 1, GROUP // ROWS)
+
+    pl.loop(0, 3)(own)
 
     position = ids_ref[...].astype(jnp.float32) / float(CORPUS)
     rate = 0.1 + 0.45 * (1.0 + jnp.cos(jnp.pi * position))
@@ -200,7 +213,6 @@
         def _():
             send(2, piece, y_down, 4, 4)
 
-        to_twin(1, piece, 2)
 
     def relay_flip(piece):
         arrive(3, piece)
@@ -210,7 +222,10 @@
             send(3, piece, y_up, 5, 6)
 
         send(3, piece, y_down, 6, 7)
-        to_twin(3, piece)
+
+        @pl.when(piece % 2 == 1)
+        def _():
+            to_twin(1, piece - 1, 3, 2)
 
     def relay_far(piece):
         arrive(4, piece)
@@ -219,15 +234,20 @@
 
     def share_last(piece):
         arrive(7, piece)
-        to_twin(7, piece)
         arrive(5, piece)
         arrive(6, piece)
-        to_twin(5, piece, 2)
+        to_twin(5, piece, 3)
 
     def take(piece, part):
         window = pl.ds(pl.multiple_of(piece * ROWS, ROWS), ROWS)
-        for slot, slots in ((8 + 4 * part, 1), (9 + 4 * part, 2), (11 + 4 * part, 1)):
-            arrive(slot, piece, slots)
+        if part == 0:
+            @pl.when(piece % 2 == 0)
+            def _():
+                arrive(8, piece, 1, 2)
+                arrive(9, piece, 3, 2)
+        else:
+            arrive(12, piece)
+            arrive(13, piece, 3)
         for at in range(4):
             slot = 4 * part + at
             to = pl.ds(slot * 2 * ROWS, 2 * ROWS)
@@ -237,37 +257,43 @@
     def give(piece, part, both):
         scores[piece, part] = both[part * 8 * ROWS:(part + 1) * 8 * ROWS]
         slots = range(4 * part, 4 * part + 4)
-        for at, slot in enumerate(slots):
-            dx, dy = STEPS[slot]
-            owner = place(dx, -dy, 0) // 2
-
-            @pl.when((piece < last) & (owner != z))
-            def _():
-                pltpu.make_async_remote_copy(
-                    src_ref=scores.at[piece, part, pl.ds(at * 2 * ROWS, 2 * ROWS), :], dst_ref=landed.at[piece, z],
-                    send_sem=out_sem.at[0], recv_sem=in_sem.at[piece],
-                    device_id={"layer": owner * 2 + side}, device_id_type=MESH,
-                ).start()
-
-            @pl.when((piece < last) & (owner == z))
-            def _():
-                landed[piece, z] = scores[piece, part, pl.ds(at * 2 * ROWS, 2 * ROWS), :]
-
-            for other in range(2):
-                target = owner * 2 + (core + other) % 2
-                block = pl.ds((at * 2 + other) * ROWS, ROWS)
-
-                @pl.when((piece == last) & (target != layer))
+        owners = [place(STEPS[slot][0], -STEPS[slot][1], 0) // 2 for slot in slots]
+
+        @pl.when(piece < last)
+        def _():
+            for at, owner in enumerate(owners):
+                block = pl.ds(at * 2 * ROWS, 2 * ROWS)
+
+                @pl.when(owner != z)
                 def _():
                     pltpu.make_async_remote_copy(
-                        src_ref=scores.at[last, part, block, :], dst_ref=direct.at[layer],
-                        send_sem=out_sem.at[1], recv_sem=in_sem.at[last],
-                        device_id={"layer": target}, device_id_type=MESH,
+                        src_ref=scores.at[piece, part, block, :], dst_ref=landed.at[piece, z],
+                        send_sem=out_sem.at[0], recv_sem=in_sem.at[piece],
+                        device_id={"layer": owner * 2 + side}, device_id_type=MESH,
                     ).start()
 
-                @pl.when((piece == last) & (target == layer))
+                @pl.when(owner == z)
                 def _():
-                    direct[layer] = scores[last, part, block, :]
+                    landed[piece, z] = scores[piece, part, block, :]
+
+        @pl.when(piece == last)
+        def _():
+            for at, owner in enumerate(owners):
+                for other in range(2):
+                    target = owner * 2 + (core + other) % 2
+                    block = pl.ds((at * 2 + other) * ROWS, ROWS)
+
+                    @pl.when(target != layer)
+                    def _():
+                        pltpu.make_async_remote_copy(
+                            src_ref=scores.at[last, part, block, :], dst_ref=direct.at[layer],
+                            send_sem=out_sem.at[1], recv_sem=in_sem.at[last],
+                            device_id={"layer": target}, device_id_type=MESH,
+                        ).start()
+
+                    @pl.when(target == layer)
+                    def _():
+                        direct[layer] = scores[last, part, block, :]
 
     kept = (core + side) % 2
 
@@ -287,6 +313,10 @@
 
     @pl.loop(0, pieces + score_behind[1])
     def _(step):
+        @pl.when(step == 2)
+        def _():
+            own(3 + step * 0)
+
         for behind, stage in stages:
             pl.when((step >= behind) & (step < pieces + behind))(functools.partial(stage, step - behind))
 
@@ -301,8 +331,8 @@
 
     by_way = [WAYS.count(way) for way in range(3)]
     sent = {3: by_way[0] + by_way[2], 4: by_way[1], 5: by_way[2], 6: by_way[0] + by_way[1]}
-    for kind in [kind for kind in range(17) if kind not in (11, 15)]:
-        block = held.at[pl.ds(0, 2 if kind in (10, 14) else 1), pl.ds(0, sent.get(kind, pieces) * ROWS), :]
+    for kind in [kind for kind in range(17) if kind not in (11, 12, 15, 16)]:
+        block = held.at[pl.ds(0, 3 if kind in (10, 14) else 1), pl.ds(0, sent.get(kind, pieces) * ROWS), :]
         pltpu.make_async_copy(block, block, send_sem.at[kind]).wait()
 
     pl.loop(0, last)(gather_depth)
@@ -336,9 +366,14 @@
     return pl.pallas_call(
         kernel,
         out_shape=jax.ShapeDtypeStruct((count, t_count), f32),
-        in_specs=[pl.BlockSpec(memory_space=pl.ANY)] * 2 + [vmem] * 4,
+        in_specs=[pl.BlockSpec(memory_space=pl.ANY)] * 6,
         out_specs=vmem,
         scratch_shapes=[
+            pltpu.VMEM(eig_out.shape[1:], f32),
+            pltpu.VMEM(eig_in.shape[1:], f32),
+            pltpu.VMEM(eig_values.shape, f32),
+            pltpu.VMEM((1, t_count), jnp.int32),
+            pltpu.SemaphoreType.DMA((4,)),
             pltpu.VMEM((16, count, flat), f32),
             pltpu.VMEM((count, flat), f32),
             pltpu.VMEM((1, t_count), f32),

time: 81.5 us -> 80.2 us (0.984)
  no operation moved by 1% of the time
where the time goes in v5:
time: 80.2 us; the launch traced here: 79.7 us
  Pallas kernels  78.2 us (98%)
  local copies, waits for them, and re-layouts  1.47 us (2%)
    pallas_call x1, Pallas kernels, shards(): pl.pallas_call(kernel, out_shape=jax.ShapeDtypeStruct((count, t_count), f...  78.2 us

profile of v5, /device:TPU:34, one launch (start us, length us, event | category | flops | bytes accessed | tf_op | source)
XLA Modules:
  0.0 79.7 jit_solution(6421521475061494542)
XLA Ops:
  0.0 78.2 %shard_map.64 = f32[64,256]{1,0:T(8,128)} custom-call(f32[64,4096]{1,0:T(8,128)} %bitcast.6, f32[256,4096]{1,0:T(8,128)} %bitcast.5, f32[64,64]{1,0:T(8,128)} %bitcast.7, f32[64,64]{1,0:T(8,128)} %bitcast.8, f32[1,4096]{1,0:T(1,128)} %values_hbm.1, s32[1,256]{1,0:T(1,128)} %bitcast.9), custom_call_target="tpu_custom_call" | custom-call | flops 6442450944 | bytes 5242880 | tf_op jit(solution)/shard_map/pallas_call | solution.py:366
  78.3 1.5 %copy.8 = f32[64,256]{1,0:T(8,128)} copy(f32[64,256]{1,0:T(8,128)} %shard_map.64) | data formatting | bytes 131072

commit v6 on v5

--- a/solution.py
+++ b/solution.py
@@ -308,7 +308,7 @@
             device_id={"layer": across}, device_id_type=MESH,
         ).start()
 
-    stages = ((0, relay_rows), (1, relay_flip), (5, relay_far), (6, share_last))
+    stages = ((0, relay_rows), (1, relay_flip), (4, relay_far), (6, share_last))
     score_behind = (6, 7)
 
     @pl.loop(0, pieces + score_behind[1])

time: 80.2 us -> 79.9 us (level)
  no operation moved by 1% of the time
where the time goes in v6:
time: 79.9 us; the launch traced here: 79.6 us
  Pallas kernels  78.1 us (98%)
  local copies, waits for them, and re-layouts  1.47 us (2%)
    pallas_call x1, Pallas kernels, shards(): pl.pallas_call(kernel, out_shape=jax.ShapeDtypeStruct((count, t_count), f...  78.1 us

profile of v6, /device:TPU:34, one launch (start us, length us, event | category | flops | bytes accessed | tf_op | source)
XLA Modules:
  0.0 79.6 jit_solution(15747278518263115119)
XLA Ops:
  0.0 78.1 %shard_map.64 = f32[64,256]{1,0:T(8,128)} custom-call(f32[64,4096]{1,0:T(8,128)} %bitcast.6, f32[256,4096]{1,0:T(8,128)} %bitcast.5, f32[64,64]{1,0:T(8,128)} %bitcast.7, f32[64,64]{1,0:T(8,128)} %bitcast.8, f32[1,4096]{1,0:T(1,128)} %values_hbm.1, s32[1,256]{1,0:T(1,128)} %bitcast.9), custom_call_target="tpu_custom_call" | custom-call | flops 6442450944 | bytes 5242880 | tf_op jit(solution)/shard_map/pallas_call | solution.py:366
  78.2 1.5 %copy.8 = f32[64,256]{1,0:T(8,128)} copy(f32[64,256]{1,0:T(8,128)} %shard_map.64) | data formatting | bytes 131072

commit v7 on v6

--- a/solution.py
+++ b/solution.py
@@ -185,13 +185,14 @@
     rate = 0.1 + 0.45 * (1.0 + jnp.cos(jnp.pi * position))
     weight[...] = rate / math.sqrt(float(q_ref.shape[1] * landed.shape[1] * 2))
 
-    t_load.wait()
-    t_count = t_ref.shape[0]
-
-    @pl.loop(0, t_ref.shape[1] // t_count)
-    def _(tile):
-        window = pl.ds(pl.multiple_of(tile * t_count, t_count), t_count)
-        t_hi[window, :], t_lo[window, :] = split(t_land[:, window].T)
+    def turn_train():
+        t_load.wait()
+        t_count = t_ref.shape[0]
+
+        @pl.loop(0, t_ref.shape[1] // t_count)
+        def _(tile):
+            window = pl.ds(pl.multiple_of(tile * t_count, t_count), t_count)
+            t_hi[window, :], t_lo[window, :] = split(t_land[:, window].T)
 
     def goes(piece, way):
         return functools.reduce(operator.or_, [piece == at for at in range(pieces) if WAYS[at] == way])
@@ -316,6 +317,8 @@
         @pl.when(step == 2)
         def _():
             own(3 + step * 0)
+
+        pl.when(step == 3)(turn_train)
 
         for behind, stage in stages:
             pl.when((step >= behind) & (step < pieces + behind))(functools.partial(stage, step - behind))

time: 79.9 us -> 79.9 us (level)
  no operation moved by 1% of the time
where the time goes in v7:
time: 79.9 us; the launch traced here: 79.6 us
  Pallas kernels  78.1 us (98%)
  local copies, waits for them, and re-layouts  1.47 us (2%)
    pallas_call x1, Pallas kernels, shards(): pl.pallas_call(kernel, out_shape=jax.ShapeDtypeStruct((count, t_count), f...  78.1 us

profile of v7, /device:TPU:34, one launch (start us, length us, event | category | flops | bytes accessed | tf_op | source)
XLA Modules:
  0.0 79.6 jit_solution(13326551355488207218)
XLA Ops:
  0.0 78.1 %shard_map.64 = f32[64,256]{1,0:T(8,128)} custom-call(f32[64,4096]{1,0:T(8,128)} %bitcast.6, f32[256,4096]{1,0:T(8,128)} %bitcast.5, f32[64,64]{1,0:T(8,128)} %bitcast.7, f32[64,64]{1,0:T(8,128)} %bitcast.8, f32[1,4096]{1,0:T(1,128)} %values_hbm.1, s32[1,256]{1,0:T(1,128)} %bitcast.9), custom_call_target="tpu_custom_call" | custom-call | flops 6442450944 | bytes 5242880 | tf_op jit(solution)/shard_map/pallas_call | solution.py:369
  78.2 1.5 %copy.8 = f32[64,256]{1,0:T(8,128)} copy(f32[64,256]{1,0:T(8,128)} %shard_map.64) | data formatting | bytes 131072
